TPU v7x, 32 devices: a whole 2x2x4 slice. The times are simulated.
32 devices in a mesh: row: 16 (over z, y, x), col: 2 (over core).
Axes of the slice: x: 2, y: 2, z: 4, core: 2. Of those that a mesh axis runs over, the one named last changes fastest.
Arguments:
- current: bfloat16 [2, 64, 8, 4, 128], P(None, 'row', 'col'), may hold values from -6 to 6
- probe: bfloat16 [2, 64, 8, 4, 128], P(None, 'row', 'col'), may hold values from -6 to 6
- near_list: int32 [64, 8, 2], P('row', 'col'), may hold values from 0 to 9, as said below
- near_blocks: bfloat16 [2, 64, 8, 2, 128, 128], P(None, 'row', 'col'), may hold values from -0.25 to 0.25
- radiation: bfloat16 [2, 128, 128], replicated, may hold values from -0.375 to 0.375
- reception: bfloat16 [2, 128, 128], replicated, may hold values from -0.375 to 0.375
- interp: float32 [256, 128], replicated, may hold values from -0.5 to 0.5
- phase: float32 [16, 256], replicated, may hold values from -3.140625 to 3.140625
- leaf_table: float32 [2, 15, 15, 128], replicated, may hold values from -0.36 to 0.36
- coarse_table: bfloat16 [2, 31, 3, 256], replicated, may hold values from -0.023925781 to 0.023925781
Outputs:
- forward_out: float32 [2, 64, 8, 4, 128], P(None, 'row', 'col')
- adjoint_out: float32 [2, 64, 8, 4, 128], P(None, 'row', 'col')
Inputs may be any that keep to these rules, and one draw needn't show every extreme that they name: `near_list`: the 2 slots of a box hold distinct codes; only slots after the first may be empty (code 9).
All inputs are finite; a program needn't handle non-finite values.
Results may differ from a plain program's by a relative error of at most 0.0027.
Values may be sent and summed in bfloat16 or wider, within the bound.
A program may use at most 128 MiB of HBM per device.

v0:
```python
import jax
import jax.numpy as jnp
from jax import lax
from jax.sharding import PartitionSpec as P

HIGH = lax.Precision.HIGHEST


def with_halo(cells, sides, width):
    for axis, dim in sides:
        count = lax.axis_size(axis)
        ends = count - 1
        head = lax.slice_in_dim(cells, 0, width, axis=dim)
        tail = lax.slice_in_dim(cells, cells.shape[dim] - width, cells.shape[dim], axis=dim)
        cells = jnp.concatenate(
            [
                lax.ppermute(tail, axis, [(i, (i + 1) % count) for i in range(ends)]),
                cells,
                lax.ppermute(head, axis, [((i + 1) % count, i) for i in range(ends)]),
            ],
            axis=dim,
        )
    return cells


def from_behind(block, axis, distance):
    devices = range(lax.axis_size(axis))
    route = [(i - distance, i) for i in devices if i - distance in devices]
    return lax.ppermute(block, axis, route)


def complex_mul(left_re, left_im, right_re, right_im):
    return (left_re * right_re - left_im * right_im, left_re * right_im + left_im * right_re)


def conj_flip(table, axes):
    flipped = jnp.flip(table, axes)
    return jnp.stack([flipped[0], -flipped[1]])


def product(form, left, right):
    return jnp.einsum(form, left, right, preferred_element_type=jnp.float32)


def near_field(current, probe, near_list, near_blocks):
    box_side = current.shape[1]
    one_hot = (near_list[..., None] == jnp.arange(9)).astype(jnp.bfloat16)
    blocks_re = near_blocks[0]
    blocks_im = near_blocks[1]
    padded = with_halo(current, (("row", 1), ("col", 2)), 1)
    shifted = jnp.stack(
        [
            padded[
                :,
                offset_code // 3 : offset_code // 3 + box_side,
                offset_code % 3 : offset_code % 3 + box_side,
            ]
            for offset_code in range(9)
        ]
    )
    picked = product("rcko,oxrcmp->xkrcmp", one_hot, shifted).astype(jnp.bfloat16)
    fwd_re = product("rckpq,krcmq->rcmp", blocks_re, picked[0]) - product(
        "rckpq,krcmq->rcmp", blocks_im, picked[1]
    )
    fwd_im = product("rckpq,krcmq->rcmp", blocks_re, picked[1]) + product(
        "rckpq,krcmq->rcmp", blocks_im, picked[0]
    )
    near_fwd = jnp.stack([fwd_re, fwd_im])
    back_re = product("rckpq,rcmp->krcmq", blocks_re, probe[0]) + product(
        "rckpq,rcmp->krcmq", blocks_im, probe[1]
    )
    back_im = product("rckpq,rcmp->krcmq", blocks_re, probe[1]) - product(
        "rckpq,rcmp->krcmq", blocks_im, probe[0]
    )
    contrib = jnp.stack([back_re, back_im])
    placed_all = jnp.einsum(
        "rcko,xkrcmp->oxrcmp", one_hot.astype(jnp.float32), contrib, precision=HIGH
    )
    placed = jnp.zeros((2, box_side + 2, box_side + 2) + contrib.shape[4:], jnp.float32)
    for offset_code in range(9):
        placed = placed.at[
            :,
            offset_code // 3 : offset_code // 3 + box_side,
            offset_code % 3 : offset_code % 3 + box_side,
        ].add(placed_all[offset_code])
    for step_dir, send_row, keep_row in ((1, box_side + 1, 1), (-1, 0, box_side)):
        arrived = from_behind(placed[:, send_row], "row", step_dir)
        placed = placed.at[:, keep_row].add(arrived)
    for step_dir, send_col, keep_col in ((1, box_side + 1, 1), (-1, 0, box_side)):
        arrived = from_behind(placed[:, 1 : box_side + 1, send_col], "col", step_dir)
        placed = placed.at[:, 1 : box_side + 1, keep_col].add(arrived)
    return (near_fwd, placed[:, 1 : box_side + 1, 1 : box_side + 1])


def far_field(vectors, rad_tab, rcv_tab, leaf_tab, coarse_tab, interp, phase):
    box_side = vectors.shape[2]
    span = 3 * box_side
    reach = 2 * box_side - 1
    out_re = product("srcmp,sqp->srcmq", vectors[:, 0], rad_tab[:, 0]) - product(
        "srcmp,sqp->srcmq", vectors[:, 1], rad_tab[:, 1]
    )
    out_im = product("srcmp,sqp->srcmq", vectors[:, 0], rad_tab[:, 1]) + product(
        "srcmp,sqp->srcmq", vectors[:, 1], rad_tab[:, 0]
    )
    leaf_out = jnp.stack([out_re, out_im], 1)
    window = with_halo(leaf_out, (("row", 2), ("col", 3)), box_side)
    offsets = jnp.arange(2 * reach + 1) - reach
    near_offset = jnp.abs(offsets) <= 1
    keep = 1.0 - (near_offset[:, None] & near_offset[None, :]).astype(jnp.float32)
    masked = leaf_tab * keep[None, None, :, :, None]
    rows_in = []
    for row_pos in range(box_side):
        cols_in = []
        for col_pos in range(box_side):
            row_first = box_side - 1 - row_pos
            col_first = box_side - 1 - col_pos
            coeffs = masked[:, :, row_first : row_first + span, col_first : col_first + span]
            part_re, part_im = complex_mul(
                coeffs[:, 0, :, :, None], coeffs[:, 1, :, :, None], window[:, 0], window[:, 1]
            )
            cols_in.append(jnp.stack([part_re.sum((1, 2)), part_im.sum((1, 2))], 1))
        rows_in.append(jnp.stack(cols_in, 2))
    leaf_in = jnp.stack(rows_in, 2)
    interpolated = jnp.einsum("kq,sxrcmq->sxrcmk", interp, leaf_out, precision=HIGH)
    angles = phase.reshape(box_side, box_side, -1)
    cos_ph = jnp.cos(angles)[:, :, None, :]
    sin_ph = jnp.sin(angles)[:, :, None, :]
    top_re = (cos_ph * interpolated[:, 0] - sin_ph * interpolated[:, 1]).sum((1, 2))
    top_im = (cos_ph * interpolated[:, 1] + sin_ph * interpolated[:, 0]).sum((1, 2))
    top_b = jnp.stack([top_re, top_im], 1).astype(jnp.bfloat16)
    row_idx = lax.axis_index("row")
    col_idx = lax.axis_index("col")
    row_count = lax.axis_size("row")
    col_count = lax.axis_size("col")
    flat_tab = coarse_tab.reshape(
        coarse_tab.shape[0], 2, coarse_tab.shape[2] * coarse_tab.shape[3], coarse_tab.shape[4]
    )
    portion = lax.all_gather(top_b[:, :, None], ("row", "col"), axis=2, tiled=True)
    sources = jnp.arange(portion.shape[2])
    src_rows = sources // col_count
    src_cols = sources % col_count
    flat_index = (row_idx - src_rows + row_count - 1) * (2 * col_count - 1) + (
        col_idx - src_cols + col_count - 1
    )
    coeff = jnp.take(flat_tab, flat_index, axis=2).astype(jnp.float32)
    distant = ((jnp.abs(row_idx - src_rows) > 1) | (jnp.abs(col_idx - src_cols) > 1)).astype(
        jnp.float32
    )
    coef_re = coeff[:, 0] * distant[None, :, None]
    coef_im = coeff[:, 1] * distant[None, :, None]
    values = portion.astype(jnp.float32)
    got_re = jnp.einsum("snq,snmq->smq", coef_re, values[:, 0], precision=HIGH) - jnp.einsum(
        "snq,snmq->smq", coef_im, values[:, 1], precision=HIGH
    )
    got_im = jnp.einsum("snq,snmq->smq", coef_re, values[:, 1], precision=HIGH) + jnp.einsum(
        "snq,snmq->smq", coef_im, values[:, 0], precision=HIGH
    )
    coarse_in = jnp.stack([got_re, got_im], 1)
    in_re = coarse_in[:, 0][:, None, None]
    in_im = coarse_in[:, 1][:, None, None]
    back_re = cos_ph * in_re + sin_ph * in_im
    back_im = cos_ph * in_im - sin_ph * in_re
    spread = jnp.einsum(
        "kq,sxrcmk->sxrcmq", interp, jnp.stack([back_re, back_im], 1), precision=HIGH
    )
    incoming = (leaf_in + spread).astype(jnp.bfloat16)
    res_re = product("srcmq,spq->srcmp", incoming[:, 0], rcv_tab[:, 0]) - product(
        "srcmq,spq->srcmp", incoming[:, 1], rcv_tab[:, 1]
    )
    res_im = product("srcmq,spq->srcmp", incoming[:, 0], rcv_tab[:, 1]) + product(
        "srcmq,spq->srcmp", incoming[:, 1], rcv_tab[:, 0]
    )
    return jnp.stack([res_re, res_im], 1)


def per_device(
    current,
    probe,
    near_list,
    near_blocks,
    radiation,
    reception,
    interp,
    phase,
    leaf_table,
    coarse_table,
):
    near_fwd, near_adj = near_field(current, probe, near_list, near_blocks)
    fwd_set = (radiation, reception, leaf_table, coarse_table)
    adj_set = (
        jnp.stack([reception[0].T, -reception[1].T]),
        jnp.stack([radiation[0].T, -radiation[1].T]),
        conj_flip(leaf_table, (1, 2)),
        conj_flip(coarse_table, (1, 2)),
    )
    far_fwd = far_field(
        current[None],
        fwd_set[0][None],
        fwd_set[1][None],
        fwd_set[2][None],
        fwd_set[3][None],
        interp,
        phase,
    )[0]
    far_adj = far_field(
        probe[None],
        adj_set[0][None],
        adj_set[1][None],
        adj_set[2][None],
        adj_set[3][None],
        interp,
        phase,
    )[0]
    return (near_fwd + far_fwd, near_adj + far_adj)


def solution(mesh):
    placed = (
        P(None, "row", "col", None, None),
        P(None, "row", "col", None, None),
        P("row", "col", None),
        P(None, "row", "col", None, None, None),
        P(),
        P(),
        P(),
        P(),
        P(),
        P(),
    )
    return jax.shard_map(
        per_device,
        mesh=mesh,
        in_specs=placed,
        out_specs=(P(None, "row", "col", None, None), P(None, "row", "col", None, None)),
        check_vma=False,
    )
```

profile of v0, /device:TPU:0, one launch (start us, length us, event | category | flops | bytes accessed | tf_op | source)
XLA Modules:
  0.0 240.7 jit_solution(15152206938238859299)
XLA Ops:
  0.7 1.0 fusion.87
  1.6 0.9 fusion.86
  2.5 0.9 fusion.13
  3.5 0.9 fusion.14
  5.1 1.3 collective-permute-start.5
  6.3 6.1 %collective-permute-start.4 = (f32[1,2,4,4,4,128]{5,4,3,2,1,0:T(4,128)}, f32[1,2,4,4,4,128]{5,4,3,2,1,0:T(4,128)}, u32[]{:S(2)}, u32[]{:S(2)}) collective-permute-start(f32[1,2,4,4,4,128]{5,4,3,2,1,0:T(4,128)} %pad_maximum_fusion.5), channel_id=1, source_target_pairs={{0,2},{2,4},{4,6},{6,8},{8,10},{10,12},{12,14},{14,16},{16,18},{18... | collective-permute-start | bytes 196616 | tf_op jit(solution)/shard_map/ppermute | solution.py:17
  12.4 1.3 fusion.127
  13.8 1.3 collective-permute-start.1
  15.0 5.4 %collective-permute-start = (bf16[2,1,4,4,128]{4,3,2,1,0:T(4,128)(2,1)}, bf16[2,1,4,4,128]{4,3,2,1,0:T(4,128)(2,1)}, u32[]{:S(2)}, u32[]{:S(2)}) collective-permute-start(bf16[2,1,4,4,128]{4,3,2,1,0:T(4,128)(2,1)} %get-tuple-element.433), channel_id=1, source_target_pairs={{0,2},{2,4},{4,6},{6,8},{8,10},{10,12},{12,14},{14,16},{16,18},{18... | collective-permute-start | bytes 24584 | tf_op jit(solution)/shard_map/ppermute | solution.py:17
  25.7 1.3 collective-permute-start.13
  28.0 1.9 fusion.120
  29.9 1.5 fusion.121
  31.4 0.9 fusion.23
  35.1 1.5 fusion.117
  36.6 1.2 fusion.118
  42.8 43.5 %all_gather.7 = bf16[1,2,32,4,256]{4,3,2,1,0:T(4,128)(2,1)S(1)} all-gather(bf16[1,2,1,4,256]{4,3,2,1,0:T(4,128)(2,1)S(1)} %pad_maximum_fusion.12), channel_id=1, replica_groups=mesh['row'=16,'col'=2] {'row','col'}, dimensions={2}, use_global_device_ids=true | all-gather | bytes 135168 | tf_op jit(solution)/shard_map/all_gather | solution.py:138
  86.3 37.0 %all_gather.6 = bf16[1,2,32,4,256]{4,3,2,1,0:T(4,128)(2,1)S(1)} all-gather(bf16[1,2,1,4,256]{4,3,2,1,0:T(4,128)(2,1)S(1)} %pad_maximum_fusion.11), channel_id=1, replica_groups=mesh['row'=16,'col'=2] {'row','col'}, dimensions={2}, use_global_device_ids=true | all-gather | bytes 135168 | tf_op jit(solution)/shard_map/all_gather | solution.py:138
  123.3 1.1 fusion
  124.4 1.1 fusion.1
  126.4 1.2 fusion.116
  129.5 0.9 fusion.75
  130.8 1.6 copy_bitcast_fusion.44
  132.5 1.6 copy_bitcast_fusion.42
  134.1 1.6 copy_bitcast_fusion.40
  135.8 1.6 copy_bitcast_fusion.32
  137.4 1.6 copy_bitcast_fusion.50
  139.1 1.6 copy_bitcast_fusion.48
  140.7 1.6 copy_bitcast_fusion.46
  142.4 1.6 copy_bitcast_fusion.34
  150.4 1.3 add_dynamic-update-slice_fusion
  151.7 1.9 fusion.54
  157.7 1.3 collective-permute-start.3
  159.0 3.2 %collective-permute-start.2 = (bf16[2,6,1,4,128]{4,3,2,1,0:T(4,128)(2,1)S(1)}, bf16[2,6,1,4,128]{4,3,2,1,0:T(4,128)(2,1)S(1)}, u32[]{:S(2)}, u32[]{:S(2)}) collective-permute-start(bf16[2,6,1,4,128]{4,3,2,1,0:T(4,128)(2,1)S(1)} %get-tuple-element.422), channel_id=1, source_target_pairs={{0,1},{2,3},{4,5},{6,7},{8,9},{10,11},{12,13},{14,15},{16,17},{18,... | collective-permute-start | bytes 36872 | tf_op jit(solution)/shard_map/ppermute | solution.py:17
  163.1 1.6 copy.524
  164.7 1.5 copy.525
  166.2 1.6 copy.522
  167.7 1.6 copy.523
  169.3 1.6 copy.520
  170.9 1.6 copy.521
  172.4 1.5 copy.512
  174.6 1.5 copy.530
  176.1 1.5 copy.531
  184.1 0.9 copy.542
  185.0 0.9 copy.543
  192.4 4.2 %collective-permute-start.12 = (f32[1,2,4,4,4,128]{5,4,3,2,1,0:T(4,128)}, f32[1,2,4,4,4,128]{5,4,3,2,1,0:T(4,128)}, u32[]{:S(2)}, u32[]{:S(2)}) collective-permute-start(f32[1,2,4,4,4,128]{5,4,3,2,1,0:T(4,128)} %pad_maximum_fusion.6), channel_id=1, source_target_pairs={{0,2},{2,4},{4,6},{6,8},{8,10},{10,12},{12,14},{14,16},{16,18},{18... | collective-permute-start | bytes 196616 | tf_op jit(solution)/shard_map/ppermute | solution.py:17
  196.6 1.9 collective-permute-start.8
  202.7 2.6 %stack.593 = bf16[9,2,4,4,4,128]{5,0,4,1,3,2:T(8,128)(2,1)S(1)} concatenate(bf16[1,2,4,4,4,128]{5,0,4,1,3,2:T(2,128)(2,1)} %copy.249, bf16[1,2,4,4,4,128]{5,0,4,1,3,2:T(2,128)(2,1)S(1)} %copy.250, bf16[1,2,4,4,4,128]{5,0,4,1,3,2:T(2,128)(2,1)} %copy.251, bf16[1,2,4,4,4,128]{5,0,4,1,3,2:T(2,128)(2,1)} %copy.252, bf16[1,2,4,4,4,128]{5,0,4,1,3,2:T(2,128)(2,1)S(1)} %copy.253, ...), dimensions={0} | concatenate | bytes 589824 | tf_op jit(solution)/shard_map/stack | solution.py:51
  205.2 1.0 fusion.2
  208.3 1.3 collective-permute-start.9
  210.1 3.9 %collective-permute-done.9 = f32[2,6,4,128]{3,2,0,1:T(4,128)S(1)} collective-permute-done((f32[2,6,4,128]{3,2,0,1:T(4,128)S(1)}, f32[2,6,4,128]{3,2,0,1:T(4,128)S(1)}, u32[]{:S(2)}, u32[]{:S(2)}) %collective-permute-start.9) | collective-permute-done | bytes 24608 | tf_op jit(solution)/shard_map/ppermute | solution.py:29
  214.0 1.3 collective-permute-start.10
  215.3 0.9 pad_maximum_fusion.2
  216.3 1.3 collective-permute-start.7
  217.6 3.0 %collective-permute-start.6 = (f32[1,2,12,4,4,128]{5,4,3,2,1,0:T(4,128)S(1)}, f32[1,2,12,4,4,128]{5,4,3,2,1,0:T(4,128)S(1)}, u32[]{:S(2)}, u32[]{:S(2)}) collective-permute-start(f32[1,2,12,4,4,128]{5,4,3,2,1,0:T(4,128)S(1)} %pad_maximum_fusion.2), channel_id=1, source_target_pairs={{0,1},{2,3},{4,5},{6,7},{8,9},{10,11},{12,13},{14,15},{16,17},{18,... | collective-permute-start | bytes 589832 | tf_op jit(solution)/shard_map/ppermute | solution.py:17
  220.7 1.3 collective-permute-start.11
  222.0 0.9 pad_maximum_fusion.3
  222.9 1.3 collective-permute-start.15
  224.2 3.0 %collective-permute-start.14 = (f32[1,2,12,4,4,128]{5,4,3,2,1,0:T(4,128)S(1)}, f32[1,2,12,4,4,128]{5,4,3,2,1,0:T(4,128)S(1)}, u32[]{:S(2)}, u32[]{:S(2)}) collective-permute-start(f32[1,2,12,4,4,128]{5,4,3,2,1,0:T(4,128)S(1)} %pad_maximum_fusion.3), channel_id=1, source_target_pairs={{0,1},{2,3},{4,5},{6,7},{8,9},{10,11},{12,13},{14,15},{16,17},{18,... | collective-permute-start | bytes 589832 | tf_op jit(solution)/shard_map/ppermute | solution.py:17
  227.4 1.2 pad_maximum_fusion
  229.7 1.2 subtract_reduce_fusion.25
  231.1 1.2 subtract_reduce_fusion.31
  233.3 1.1 pad_maximum_fusion.1
  235.4 1.2 subtract_reduce_fusion.9
  236.8 1.2 subtract_reduce_fusion.15
  (432 shorter events, 54.1 us)
Async XLA Ops:
  0.6 26.3 %copy-start = (f32[256,128]{1,0:T(8,128)S(1)}, f32[256,128]{1,0:T(8,128)}, u32[]{:S(2)}) copy-start(f32[256,128]{1,0:T(8,128)} %param.44) | copy-start | bytes 393220
  0.6 27.0 %copy-start.2 = (f32[2,15,15,128]{3,0,2,1:T(2,128)S(1)}, f32[2,15,15,128]{3,0,2,1:T(2,128)}, u32[]{:S(2)}) copy-start(f32[2,15,15,128]{3,0,2,1:T(2,128)} %param.46) | copy-start | bytes 691204
  5.1 210.3 %collective-permute-start.5 = (f32[1,2,4,4,4,128]{5,4,3,2,1,0:T(4,128)}, f32[1,2,4,4,4,128]{5,4,3,2,1,0:T(4,128)}, u32[]{:S(2)}, u32[]{:S(2)}) collective-permute-start(f32[1,2,4,4,4,128]{5,4,3,2,1,0:T(4,128)} %pad_maximum_fusion.5), channel_id=1, source_target_pairs={{2,0},{4,2},{6,4},{8,6},{10,8},{12,10},{14,12},{16,14},{18,16},{20... | collective-permute-start | bytes 196616 | tf_op jit(solution)/shard_map/ppermute | solution.py:19
  6.3 209.0 %collective-permute-start.4 = (f32[1,2,4,4,4,128]{5,4,3,2,1,0:T(4,128)}, f32[1,2,4,4,4,128]{5,4,3,2,1,0:T(4,128)}, u32[]{:S(2)}, u32[]{:S(2)}) collective-permute-start(f32[1,2,4,4,4,128]{5,4,3,2,1,0:T(4,128)} %pad_maximum_fusion.5), channel_id=1, source_target_pairs={{0,2},{2,4},{4,6},{6,8},{8,10},{10,12},{12,14},{14,16},{16,18},{18... | collective-permute-start | bytes 196616 | tf_op jit(solution)/shard_map/ppermute | solution.py:17
  13.8 143.2 %collective-permute-start.1 = (bf16[2,1,4,4,128]{4,3,2,1,0:T(4,128)(2,1)}, bf16[2,1,4,4,128]{4,3,2,1,0:T(4,128)(2,1)S(1)}, u32[]{:S(2)}, u32[]{:S(2)}) collective-permute-start(bf16[2,1,4,4,128]{4,3,2,1,0:T(4,128)(2,1)} %get-tuple-element.432), channel_id=1, source_target_pairs={{2,0},{4,2},{6,4},{8,6},{10,8},{12,10},{14,12},{16,14},{18,16},{20... | collective-permute-start | bytes 24584 | tf_op jit(solution)/shard_map/ppermute | solution.py:19
  15.0 141.2 %collective-permute-start = (bf16[2,1,4,4,128]{4,3,2,1,0:T(4,128)(2,1)}, bf16[2,1,4,4,128]{4,3,2,1,0:T(4,128)(2,1)}, u32[]{:S(2)}, u32[]{:S(2)}) collective-permute-start(bf16[2,1,4,4,128]{4,3,2,1,0:T(4,128)(2,1)} %get-tuple-element.433), channel_id=1, source_target_pairs={{0,2},{2,4},{4,6},{6,8},{8,10},{10,12},{12,14},{14,16},{16,18},{18... | collective-permute-start | bytes 24584 | tf_op jit(solution)/shard_map/ppermute | solution.py:17
  25.7 196.3 %collective-permute-start.13 = (f32[1,2,4,4,4,128]{5,4,3,2,1,0:T(4,128)}, f32[1,2,4,4,4,128]{5,4,3,2,1,0:T(4,128)}, u32[]{:S(2)}, u32[]{:S(2)}) collective-permute-start(f32[1,2,4,4,4,128]{5,4,3,2,1,0:T(4,128)} %pad_maximum_fusion.6), channel_id=1, source_target_pairs={{2,0},{4,2},{6,4},{8,6},{10,8},{12,10},{14,12},{16,14},{18,16},{20... | collective-permute-start | bytes 196616 | tf_op jit(solution)/shard_map/ppermute | solution.py:19
  38.0 87.6 %copy-start.115 = (s32[4,4,2]{2,1,0:T(4,128)}, s32[4,4,2]{2,1,0:T(4,128)S(1)}, u32[]{:S(2)}) copy-start(s32[4,4,2]{2,1,0:T(4,128)S(1)} %copy.258) | copy-start | bytes 388
  126.4 16.0 %copy-start.80 = (f32[1,1,12,12,128]{4,1,3,2,0:T(1,128)S(1)}, f32[1,1,12,12,128]{4,1,3,2,0:T(1,128)}, u32[]{:S(2)}) copy-start(f32[1,1,12,12,128]{4,1,3,2,0:T(1,128)} %get-tuple-element.371) | copy-start | bytes 221188
  127.5 16.5 %copy-start.78 = (f32[1,1,12,12,128]{4,1,3,2,0:T(1,128)S(1)}, f32[1,1,12,12,128]{4,1,3,2,0:T(1,128)}, u32[]{:S(2)}) copy-start(f32[1,1,12,12,128]{4,1,3,2,0:T(1,128)} %get-tuple-element.373) | copy-start | bytes 221188
  127.5 16.5 %copy-start.79 = (f32[1,1,12,12,128]{4,1,3,2,0:T(1,128)S(1)}, f32[1,1,12,12,128]{4,1,3,2,0:T(1,128)}, u32[]{:S(2)}) copy-start(f32[1,1,12,12,128]{4,1,3,2,0:T(1,128)} %get-tuple-element.374) | copy-start | bytes 221188
  127.5 17.2 %copy-start.76 = (f32[1,1,12,12,128]{4,1,3,2,0:T(1,128)S(1)}, f32[1,1,12,12,128]{4,1,3,2,0:T(1,128)}, u32[]{:S(2)}) copy-start(f32[1,1,12,12,128]{4,1,3,2,0:T(1,128)} %get-tuple-element.375) | copy-start | bytes 221188
  127.5 17.2 %copy-start.77 = (f32[1,1,12,12,128]{4,1,3,2,0:T(1,128)S(1)}, f32[1,1,12,12,128]{4,1,3,2,0:T(1,128)}, u32[]{:S(2)}) copy-start(f32[1,1,12,12,128]{4,1,3,2,0:T(1,128)} %get-tuple-element.376) | copy-start | bytes 221188
  129.5 15.8 %copy-start.99 = (f32[1,1,12,12,128]{4,1,3,2,0:T(1,128)S(1)}, f32[1,1,12,12,128]{4,1,3,2,0:T(1,128)}, u32[]{:S(2)}) copy-start(f32[1,1,12,12,128]{4,1,3,2,0:T(1,128)} %get-tuple-element.397) | copy-start | bytes 221188
  129.5 15.8 %copy-start.100 = (f32[1,1,12,12,128]{4,1,3,2,0:T(1,128)S(1)}, f32[1,1,12,12,128]{4,1,3,2,0:T(1,128)}, u32[]{:S(2)}) copy-start(f32[1,1,12,12,128]{4,1,3,2,0:T(1,128)} %get-tuple-element.398) | copy-start | bytes 221188
  130.6 15.5 %copy-start.75 = (f32[1,1,12,12,128]{4,1,3,2,0:T(1,128)S(1)}, f32[1,1,12,12,128]{4,1,3,2,0:T(1,128)}, u32[]{:S(2)}) copy-start(f32[1,1,12,12,128]{4,1,3,2,0:T(1,128)} %get-tuple-element.368) | copy-start | bytes 221188
  130.8 16.0 %copy-start.96 = (f32[1,1,12,12,128]{4,1,3,2,0:T(1,128)S(1)}, f32[1,1,12,12,128]{4,1,3,2,0:T(1,128)}, u32[]{:S(2)}) copy-start(f32[1,1,12,12,128]{4,1,3,2,0:T(1,128)} %get-tuple-element.387) | copy-start | bytes 221188
  130.8 16.0 %copy-start.97 = (f32[1,1,12,12,128]{4,1,3,2,0:T(1,128)S(1)}, f32[1,1,12,12,128]{4,1,3,2,0:T(1,128)}, u32[]{:S(2)}) copy-start(f32[1,1,12,12,128]{4,1,3,2,0:T(1,128)} %get-tuple-element.396) | copy-start | bytes 221188
  148.9 25.1 %copy-start.74 = (f32[1,1,12,12,128]{4,0,3,2,1:T(1,128)S(1)}, f32[1,1,12,12,128]{4,0,3,2,1:T(1,128)}, u32[]{:S(2)}) copy-start(f32[1,1,12,12,128]{4,0,3,2,1:T(1,128)} %get-tuple-element.336) | copy-start | bytes 221188
  150.4 27.3 %copy-start.73 = (f32[1,1,12,12,128]{4,0,3,2,1:T(1,128)S(1)}, f32[1,1,12,12,128]{4,0,3,2,1:T(1,128)}, u32[]{:S(2)}) copy-start(f32[1,1,12,12,128]{4,0,3,2,1:T(1,128)} %get-tuple-element.351) | copy-start | bytes 221188
  151.7 26.6 %copy-start.72 = (f32[1,1,12,12,128]{4,0,3,2,1:T(1,128)S(1)}, f32[1,1,12,12,128]{4,0,3,2,1:T(1,128)}, u32[]{:S(2)}) copy-start(f32[1,1,12,12,128]{4,0,3,2,1:T(1,128)} %get-tuple-element.352) | copy-start | bytes 221188
  153.7 25.3 %copy-start.71 = (f32[1,1,12,12,128]{4,0,3,2,1:T(1,128)S(1)}, f32[1,1,12,12,128]{4,0,3,2,1:T(1,128)}, u32[]{:S(2)}) copy-start(f32[1,1,12,12,128]{4,0,3,2,1:T(1,128)} %get-tuple-element.349) | copy-start | bytes 221188
  153.7 25.9 %copy-start.70 = (f32[1,1,12,12,128]{4,0,3,2,1:T(1,128)S(1)}, f32[1,1,12,12,128]{4,0,3,2,1:T(1,128)}, u32[]{:S(2)}) copy-start(f32[1,1,12,12,128]{4,0,3,2,1:T(1,128)} %get-tuple-element.350) | copy-start | bytes 221188
  153.8 26.4 %copy-start.69 = (f32[1,1,12,12,128]{4,0,3,2,1:T(1,128)S(1)}, f32[1,1,12,12,128]{4,0,3,2,1:T(1,128)}, u32[]{:S(2)}) copy-start(f32[1,1,12,12,128]{4,0,3,2,1:T(1,128)} %get-tuple-element.337) | copy-start | bytes 221188
  157.7 28.2 %copy-start.89 = (f32[1,1,12,12,128]{4,0,3,2,1:T(1,128)S(1)}, f32[1,1,12,12,128]{4,0,3,2,1:T(1,128)}, u32[]{:S(2)}) copy-start(f32[1,1,12,12,128]{4,0,3,2,1:T(1,128)} %get-tuple-element.362) | copy-start | bytes 221188
  157.7 34.7 %collective-permute-start.3 = (bf16[2,6,1,4,128]{4,3,2,1,0:T(4,128)(2,1)S(1)}, bf16[2,6,1,4,128]{4,3,2,1,0:T(4,128)(2,1)S(1)}, u32[]{:S(2)}, u32[]{:S(2)}) collective-permute-start(bf16[2,6,1,4,128]{4,3,2,1,0:T(4,128)(2,1)S(1)} %get-tuple-element.421), channel_id=1, source_target_pairs={{1,0},{3,2},{5,4},{7,6},{9,8},{11,10},{13,12},{15,14},{17,16},{19,... | collective-permute-start | bytes 36872 | tf_op jit(solution)/shard_map/ppermute | solution.py:19
  159.0 37.6 %collective-permute-start.2 = (bf16[2,6,1,4,128]{4,3,2,1,0:T(4,128)(2,1)S(1)}, bf16[2,6,1,4,128]{4,3,2,1,0:T(4,128)(2,1)S(1)}, u32[]{:S(2)}, u32[]{:S(2)}) collective-permute-start(bf16[2,6,1,4,128]{4,3,2,1,0:T(4,128)(2,1)S(1)} %get-tuple-element.422), channel_id=1, source_target_pairs={{0,1},{2,3},{4,5},{6,7},{8,9},{10,11},{12,13},{14,15},{16,17},{18,... | collective-permute-start | bytes 36872 | tf_op jit(solution)/shard_map/ppermute | solution.py:17
  162.2 23.6 %copy-start.88 = (f32[1,1,12,12,128]{4,0,3,2,1:T(1,128)S(1)}, f32[1,1,12,12,128]{4,0,3,2,1:T(1,128)}, u32[]{:S(2)}) copy-start(f32[1,1,12,12,128]{4,0,3,2,1:T(1,128)} %get-tuple-element.363) | copy-start | bytes 221188
  163.1 23.4 %copy-start.87 = (f32[1,1,12,12,128]{4,0,3,2,1:T(1,128)S(1)}, f32[1,1,12,12,128]{4,0,3,2,1:T(1,128)}, u32[]{:S(2)}) copy-start(f32[1,1,12,12,128]{4,0,3,2,1:T(1,128)} %get-tuple-element.353) | copy-start | bytes 221188
  166.2 21.6 %copy-start.86 = (f32[1,1,12,12,128]{4,0,3,2,1:T(1,128)S(1)}, f32[1,1,12,12,128]{4,0,3,2,1:T(1,128)}, u32[]{:S(2)}) copy-start(f32[1,1,12,12,128]{4,0,3,2,1:T(1,128)} %get-tuple-element.356) | copy-start | bytes 221188
  167.7 20.7 %copy-start.85 = (f32[1,1,12,12,128]{4,0,3,2,1:T(1,128)S(1)}, f32[1,1,12,12,128]{4,0,3,2,1:T(1,128)}, u32[]{:S(2)}) copy-start(f32[1,1,12,12,128]{4,0,3,2,1:T(1,128)} %get-tuple-element.357) | copy-start | bytes 221188
  169.3 19.8 %copy-start.84 = (f32[1,1,12,12,128]{4,0,3,2,1:T(1,128)S(1)}, f32[1,1,12,12,128]{4,0,3,2,1:T(1,128)}, u32[]{:S(2)}) copy-start(f32[1,1,12,12,128]{4,0,3,2,1:T(1,128)} %get-tuple-element.358) | copy-start | bytes 221188
  170.9 18.9 %copy-start.83 = (f32[1,1,12,12,128]{4,0,3,2,1:T(1,128)S(1)}, f32[1,1,12,12,128]{4,0,3,2,1:T(1,128)}, u32[]{:S(2)}) copy-start(f32[1,1,12,12,128]{4,0,3,2,1:T(1,128)} %get-tuple-element.359) | copy-start | bytes 221188
  172.4 18.0 %copy-start.82 = (f32[1,1,12,12,128]{4,0,3,2,1:T(1,128)S(1)}, f32[1,1,12,12,128]{4,0,3,2,1:T(1,128)}, u32[]{:S(2)}) copy-start(f32[1,1,12,12,128]{4,0,3,2,1:T(1,128)} %get-tuple-element.360) | copy-start | bytes 221188
  174.0 17.1 %copy-start.81 = (f32[1,1,12,12,128]{4,0,3,2,1:T(1,128)S(1)}, f32[1,1,12,12,128]{4,0,3,2,1:T(1,128)}, u32[]{:S(2)}) copy-start(f32[1,1,12,12,128]{4,0,3,2,1:T(1,128)} %get-tuple-element.361) | copy-start | bytes 221188
  192.4 29.5 %collective-permute-start.12 = (f32[1,2,4,4,4,128]{5,4,3,2,1,0:T(4,128)}, f32[1,2,4,4,4,128]{5,4,3,2,1,0:T(4,128)}, u32[]{:S(2)}, u32[]{:S(2)}) collective-permute-start(f32[1,2,4,4,4,128]{5,4,3,2,1,0:T(4,128)} %pad_maximum_fusion.6), channel_id=1, source_target_pairs={{0,2},{2,4},{4,6},{6,8},{8,10},{10,12},{12,14},{14,16},{16,18},{18... | collective-permute-start | bytes 196616 | tf_op jit(solution)/shard_map/ppermute | solution.py:17
  196.6 10.9 %collective-permute-start.8 = (f32[2,6,4,128]{3,2,0,1:T(4,128)}, f32[2,6,4,128]{3,2,0,1:T(4,128)}, u32[]{:S(2)}, u32[]{:S(2)}) collective-permute-start(f32[2,6,4,128]{3,2,0,1:T(4,128)} %slice_bitcast_fusion.41), channel_id=1, source_target_pairs={{0,2},{2,4},{4,6},{6,8},{8,10},{10,12},{12,14},{14,16},{16,18},{18... | collective-permute-start | bytes 73736 | tf_op jit(solution)/shard_map/ppermute | solution.py:29
  207.0 21.6 %copy-start.58 = (f32[12,12,128]{2,1,0:T(8,128)S(1)}, f32[12,12,128]{2,1,0:T(8,128)}, u32[]{:S(2)}) copy-start(f32[12,12,128]{2,1,0:T(8,128)} %get-tuple-element.455) | copy-start | bytes 221188
  207.0 21.6 %copy-start.59 = (f32[12,12,128]{2,1,0:T(8,128)S(1)}, f32[12,12,128]{2,1,0:T(8,128)}, u32[]{:S(2)}) copy-start(f32[12,12,128]{2,1,0:T(8,128)} %get-tuple-element.456) | copy-start | bytes 221188
  207.0 21.6 %copy-start.63 = (f32[12,12,128]{2,1,0:T(8,128)S(1)}, f32[12,12,128]{2,1,0:T(8,128)}, u32[]{:S(2)}) copy-start(f32[12,12,128]{2,1,0:T(8,128)} %get-tuple-element.453) | copy-start | bytes 221188
  207.0 21.6 %copy-start.64 = (f32[12,12,128]{2,1,0:T(8,128)S(1)}, f32[12,12,128]{2,1,0:T(8,128)}, u32[]{:S(2)}) copy-start(f32[12,12,128]{2,1,0:T(8,128)} %get-tuple-element.454) | copy-start | bytes 221188
  207.1 21.6 %copy-start.65 = (f32[12,12,128]{2,1,0:T(8,128)S(1)}, f32[12,12,128]{2,1,0:T(8,128)}, u32[]{:S(2)}) copy-start(f32[12,12,128]{2,1,0:T(8,128)} %get-tuple-element.451) | copy-start | bytes 221188
  207.1 21.6 %copy-start.66 = (f32[12,12,128]{2,1,0:T(8,128)S(1)}, f32[12,12,128]{2,1,0:T(8,128)}, u32[]{:S(2)}) copy-start(f32[12,12,128]{2,1,0:T(8,128)} %get-tuple-element.452) | copy-start | bytes 221188
  207.1 21.6 %copy-start.67 = (f32[12,12,128]{2,1,0:T(8,128)S(1)}, f32[12,12,128]{2,1,0:T(8,128)}, u32[]{:S(2)}) copy-start(f32[12,12,128]{2,1,0:T(8,128)} %get-tuple-element.443) | copy-start | bytes 221188
  207.1 21.6 %copy-start.68 = (f32[12,12,128]{2,1,0:T(8,128)S(1)}, f32[12,12,128]{2,1,0:T(8,128)}, u32[]{:S(2)}) copy-start(f32[12,12,128]{2,1,0:T(8,128)} %get-tuple-element.444) | copy-start | bytes 221188
  208.3 5.7 %collective-permute-start.9 = (f32[2,6,4,128]{3,2,0,1:T(4,128)S(1)}, f32[2,6,4,128]{3,2,0,1:T(4,128)S(1)}, u32[]{:S(2)}, u32[]{:S(2)}) collective-permute-start(f32[2,6,4,128]{3,2,0,1:T(4,128)S(1)} %slice_bitcast_fusion.40), channel_id=1, source_target_pairs={{2,0},{4,2},{6,4},{8,6},{10,8},{12,10},{14,12},{16,14},{18,16},{20... | collective-permute-start | bytes 73736 | tf_op jit(solution)/shard_map/ppermute | solution.py:29
  209.9 19.6 %copy-start.32 = (f32[12,12,128]{2,1,0:T(8,128)S(1)}, f32[12,12,128]{2,1,0:T(8,128)}, u32[]{:S(2)}) copy-start(f32[12,12,128]{2,1,0:T(8,128)} %get-tuple-element.461) | copy-start | bytes 221188
  209.9 19.6 %copy-start.33 = (f32[12,12,128]{2,1,0:T(8,128)S(1)}, f32[12,12,128]{2,1,0:T(8,128)}, u32[]{:S(2)}) copy-start(f32[12,12,128]{2,1,0:T(8,128)} %get-tuple-element.462) | copy-start | bytes 221188
  209.9 19.6 %copy-start.37 = (f32[12,12,128]{2,1,0:T(8,128)S(1)}, f32[12,12,128]{2,1,0:T(8,128)}, u32[]{:S(2)}) copy-start(f32[12,12,128]{2,1,0:T(8,128)} %get-tuple-element.459) | copy-start | bytes 221188
  210.0 19.6 %copy-start.38 = (f32[12,12,128]{2,1,0:T(8,128)S(1)}, f32[12,12,128]{2,1,0:T(8,128)}, u32[]{:S(2)}) copy-start(f32[12,12,128]{2,1,0:T(8,128)} %get-tuple-element.460) | copy-start | bytes 221188
  210.0 19.6 %copy-start.42 = (f32[12,12,128]{2,1,0:T(8,128)S(1)}, f32[12,12,128]{2,1,0:T(8,128)}, u32[]{:S(2)}) copy-start(f32[12,12,128]{2,1,0:T(8,128)} %get-tuple-element.457) | copy-start | bytes 221188
  210.0 19.6 %copy-start.43 = (f32[12,12,128]{2,1,0:T(8,128)S(1)}, f32[12,12,128]{2,1,0:T(8,128)}, u32[]{:S(2)}) copy-start(f32[12,12,128]{2,1,0:T(8,128)} %get-tuple-element.458) | copy-start | bytes 221188
  210.0 19.6 %copy-start.47 = (f32[12,12,128]{2,1,0:T(8,128)S(1)}, f32[12,12,128]{2,1,0:T(8,128)}, u32[]{:S(2)}) copy-start(f32[12,12,128]{2,1,0:T(8,128)} %get-tuple-element.445) | copy-start | bytes 221188
  210.0 19.6 %copy-start.48 = (f32[12,12,128]{2,1,0:T(8,128)S(1)}, f32[12,12,128]{2,1,0:T(8,128)}, u32[]{:S(2)}) copy-start(f32[12,12,128]{2,1,0:T(8,128)} %get-tuple-element.446) | copy-start | bytes 221188
  210.0 19.6 %copy-start.49 = (f32[12,12,128]{2,1,0:T(8,128)S(1)}, f32[12,12,128]{2,1,0:T(8,128)}, u32[]{:S(2)}) copy-start(f32[12,12,128]{2,1,0:T(8,128)} %get-tuple-element.447) | copy-start | bytes 221188
  210.0 19.6 %copy-start.50 = (f32[12,12,128]{2,1,0:T(8,128)S(1)}, f32[12,12,128]{2,1,0:T(8,128)}, u32[]{:S(2)}) copy-start(f32[12,12,128]{2,1,0:T(8,128)} %get-tuple-element.448) | copy-start | bytes 221188
  210.0 19.6 %copy-start.51 = (f32[12,12,128]{2,1,0:T(8,128)S(1)}, f32[12,12,128]{2,1,0:T(8,128)}, u32[]{:S(2)}) copy-start(f32[12,12,128]{2,1,0:T(8,128)} %get-tuple-element.449) | copy-start | bytes 221188
  210.0 19.6 %copy-start.52 = (f32[12,12,128]{2,1,0:T(8,128)S(1)}, f32[12,12,128]{2,1,0:T(8,128)}, u32[]{:S(2)}) copy-start(f32[12,12,128]{2,1,0:T(8,128)} %get-tuple-element.450) | copy-start | bytes 221188
  214.0 6.6 %collective-permute-start.10 = (f32[2,4,4,128]{3,2,0,1:T(4,128)S(1)}, f32[2,4,4,128]{3,2,0,1:T(4,128)S(1)}, u32[]{:S(2)}, u32[]{:S(2)}) collective-permute-start(f32[2,4,4,128]{3,2,0,1:T(4,128)S(1)} %slice_bitcast_fusion.47), channel_id=1, source_target_pairs={{0,1},{2,3},{4,5},{6,7},{8,9},{10,11},{12,13},{14,15},{16,17},{18,... | collective-permute-start | bytes 49160 | tf_op jit(solution)/shard_map/ppermute | solution.py:29
  216.3 11.2 %collective-permute-start.7 = (f32[1,2,12,4,4,128]{5,4,3,2,1,0:T(4,128)S(1)}, f32[1,2,12,4,4,128]{5,4,3,2,1,0:T(4,128)S(1)}, u32[]{:S(2)}, u32[]{:S(2)}) collective-permute-start(f32[1,2,12,4,4,128]{5,4,3,2,1,0:T(4,128)S(1)} %pad_maximum_fusion.2), channel_id=1, source_target_pairs={{1,0},{3,2},{5,4},{7,6},{9,8},{11,10},{13,12},{15,14},{17,16},{19,... | collective-permute-start | bytes 589832 | tf_op jit(solution)/shard_map/ppermute | solution.py:19
  217.6 9.9 %collective-permute-start.6 = (f32[1,2,12,4,4,128]{5,4,3,2,1,0:T(4,128)S(1)}, f32[1,2,12,4,4,128]{5,4,3,2,1,0:T(4,128)S(1)}, u32[]{:S(2)}, u32[]{:S(2)}) collective-permute-start(f32[1,2,12,4,4,128]{5,4,3,2,1,0:T(4,128)S(1)} %pad_maximum_fusion.2), channel_id=1, source_target_pairs={{0,1},{2,3},{4,5},{6,7},{8,9},{10,11},{12,13},{14,15},{16,17},{18,... | collective-permute-start | bytes 589832 | tf_op jit(solution)/shard_map/ppermute | solution.py:17
  220.7 6.6 %collective-permute-start.11 = (f32[2,4,4,128]{3,2,0,1:T(4,128)S(1)}, f32[2,4,4,128]{3,2,0,1:T(4,128)S(1)}, u32[]{:S(2)}, u32[]{:S(2)}) collective-permute-start(f32[2,4,4,128]{3,2,0,1:T(4,128)S(1)} %slice_bitcast_fusion.46), channel_id=1, source_target_pairs={{1,0},{3,2},{5,4},{7,6},{9,8},{11,10},{13,12},{15,14},{17,16},{19,... | collective-permute-start | bytes 49160 | tf_op jit(solution)/shard_map/ppermute | solution.py:29
  222.9 10.4 %collective-permute-start.15 = (f32[1,2,12,4,4,128]{5,4,3,2,1,0:T(4,128)S(1)}, f32[1,2,12,4,4,128]{5,4,3,2,1,0:T(4,128)S(1)}, u32[]{:S(2)}, u32[]{:S(2)}) collective-permute-start(f32[1,2,12,4,4,128]{5,4,3,2,1,0:T(4,128)S(1)} %pad_maximum_fusion.3), channel_id=1, source_target_pairs={{1,0},{3,2},{5,4},{7,6},{9,8},{11,10},{13,12},{15,14},{17,16},{19,... | collective-permute-start | bytes 589832 | tf_op jit(solution)/shard_map/ppermute | solution.py:19
  224.2 9.1 %collective-permute-start.14 = (f32[1,2,12,4,4,128]{5,4,3,2,1,0:T(4,128)S(1)}, f32[1,2,12,4,4,128]{5,4,3,2,1,0:T(4,128)S(1)}, u32[]{:S(2)}, u32[]{:S(2)}) collective-permute-start(f32[1,2,12,4,4,128]{5,4,3,2,1,0:T(4,128)S(1)} %pad_maximum_fusion.3), channel_id=1, source_target_pairs={{0,1},{2,3},{4,5},{6,7},{8,9},{10,11},{12,13},{14,15},{16,17},{18,... | collective-permute-start | bytes 589832 | tf_op jit(solution)/shard_map/ppermute | solution.py:17
  (73 other events, 414.2 us)
where the time goes:
time: 243 us; the launch traced here: 241 us
  blocking collectives  80.5 us (33%)
  local copies, waits for them, and re-layouts  72.9 us (30%)
  starting transfers between devices  38.5 us (16%)
  other arithmetic  25 us (10%)
  matrix products  16.8 us (7%)
  waiting for transfers between devices  3.97 us (2%)
  between operations  2.88 us (1%)
    all_gather x2, blocking collectives, far_field(): lax.all_gather(top_b[:, :, None], ('row', 'col'), axis=2, tiled=True)  80.5 us
    unnamed x297, local copies, waits for them, and re-layouts  50.4 us
    ppermute x6, starting transfers between devices, with_halo(): lax.ppermute(tail, axis, [(i, (i + 1) % count) for i in range(ends)])  25 us
    dot_general x25, matrix products, product(): return jnp.einsum(form, left, right, preferred_element_type=jnp.float32)  14.8 us
    ppermute x6, starting transfers between devices, with_halo(): lax.ppermute(head, axis, [((i + 1) % count, i) for i in range(ends)])  7.72 us
    another operation x10, local copies, waits for them, and re-layouts, near_field(): jnp.stack([padded[:, offset_code // 3:offset_code // 3 + box_side, offset...  7.41 us
    reduce_sum x6, other arithmetic, far_field(): cols_in.append(jnp.stack([part_re.sum((1, 2)), part_im.sum((1, 2))], 1))  6.17 us
    ppermute x4, starting transfers between devices, from_behind(): return lax.ppermute(block, axis, route)  5.79 us
  transfers between devices with their start and end apart: 16, of which 1 were waited for; matrix products, arithmetic and copies ran while one was open for 43% of the time, Pallas kernels for 0%

commit v1 on v0

v1 whole, which is shorter than its diff:
```python
import functools

import jax
import jax.numpy as jnp
from jax import lax
from jax.experimental import pallas as pl
from jax.experimental.pallas import tpu as pltpu
from jax.sharding import PartitionSpec as P

HIGH = lax.Precision.HIGHEST
F32 = jnp.float32
BF16 = jnp.bfloat16
MESH = pl.DeviceIdType.MESH


def upper(shape):
    return lax.broadcasted_iota(jnp.int32, shape, len(shape) - 2) < 4


def swap(x):
    turned = pltpu.roll(x, 4, x.ndim - 2)
    return jnp.where(upper(x.shape), -turned, turned)


def interleave(re, im):
    low = upper(re.shape)
    return jnp.where(low, re, pltpu.roll(im, 4, 1)), jnp.where(low, pltpu.roll(re, 4, 1), im)


def nn(a, b, precision=None):
    return lax.dot_general(a, b, (((1,), (0,)), ((), ())), precision=precision, preferred_element_type=F32)


def nt(a, b, precision=None):
    return lax.dot_general(a, b, (((1,), (1,)), ((), ())), precision=precision, preferred_element_type=F32)


def kernel(
    n_row,
    n_col,
    cur,
    prb,
    codes,
    near_hbm,
    rad,
    rec,
    interp,
    phase,
    leaf_tab,
    coarse_tab,
    out_fwd,
    out_adj,
    halo,
    gath,
    near,
    w_rad,
    w_rcv,
    tab,
    patt,
    leaf,
    vec,
    window,
    placed,
    ring_out,
    ring_in,
    near_fwd,
    back,
    trig,
    near_sem,
    halo_send,
    halo_recv,
    ring_send,
    ring_recv,
    all_send,
    all_recv,
):
    row = lax.axis_index("row")
    col = lax.axis_index("col")
    total = n_row * n_col
    me = row * n_col + col

    barrier = pltpu.get_barrier_semaphore()

    def greet(n, carry):
        @pl.when(n != me)
        def _():
            pl.semaphore_signal(barrier, inc=1, device_id=(n // n_col, n % n_col), device_id_type=MESH)

        return carry

    lax.fori_loop(0, total, greet, 0)
    load_near = pltpu.make_async_copy(near_hbm, near, near_sem)
    load_near.start()

    halo[4, 0:128] = cur[...]
    halo[4, 128:256] = prb[...]
    for x in range(2):
        sign = 1.0 if x == 0 else -1.0
        cols = slice(128 * x, 128 * x + 128)
        rad_f = rad[x].astype(F32)
        rec_f = rec[x].astype(F32)
        w_rad[0, :, cols] = rad_f.T.astype(BF16)
        w_rad[1, :, cols] = (rec_f * sign).astype(BF16)
        w_rcv[0, :, cols] = rec_f.T.astype(BF16)
        w_rcv[1, :, cols] = (rad_f * sign).astype(BF16)
    angles = phase[...]
    trig[0] = jnp.cos(angles)
    trig[1] = jnp.sin(angles)

    def patterns(slot):
        for s in range(2):
            both = nn(halo[slot, 128 * s : 128 * s + 128], w_rad[s])
            re = (both[:64, :128] - both[64:, 128:]).reshape(8, 8, 128)
            im = (both[64:, :128] + both[:64, 128:]).reshape(8, 8, 128)
            even, odd = interleave(re, im)
            patt[s, 0, :, 0] = even
            patt[s, 0, :, 1] = odd
            patt[s, 1, :, 0] = swap(even) if s == 0 else -swap(even)
            patt[s, 1, :, 1] = swap(odd) if s == 0 else -swap(odd)

    def boxes_of(slot, s):
        base = 128 * s
        re = halo[slot, base : base + 64].astype(F32).reshape(8, 8, 128)
        im = halo[slot, base + 64 : base + 128].astype(F32).reshape(8, 8, 128)
        return interleave(re, im)

    patterns(4)
    for s in range(2):
        own = patt[s, 0].reshape(128, 128)
        wide = nt(own, interp[...], HIGH).reshape(16, 8, 256)
        cos_sum = jnp.zeros((8, 256), F32)
        sin_sum = jnp.zeros((8, 256), F32)
        for j in range(16):
            cos_sum += trig[0, j : j + 1] * wide[j]
            sin_sum += trig[1, j : j + 1] * wide[j]
        top = cos_sum + swap(sin_sum)
        vec[0, s] = top
    gath[me] = vec[0].reshape(16, 256).astype(BF16)

    pl.semaphore_wait(barrier, total - 1)

    def halo_copy(d):
        dr = d // 3 - 1
        dc = d % 3 - 1
        return pltpu.make_async_remote_copy(
            src_ref=halo.at[4],
            dst_ref=halo.at[8 - d],
            send_sem=halo_send.at[d],
            recv_sem=halo_recv.at[8 - d],
            device_id=(row + dr, col + dc),
            device_id_type=MESH,
        )

    def exists(d):
        r = row + d // 3 - 1
        c = col + d % 3 - 1
        return (d != 4) & (r >= 0) & (r < n_row) & (c >= 0) & (c < n_col)

    def send_halo(d, carry):
        @pl.when(exists(d))
        def _():
            halo_copy(d).start()

        return carry

    lax.fori_loop(0, 9, send_halo, 0)

    def send_top(n, carry):
        @pl.when(n != me)
        def _():
            pltpu.make_async_remote_copy(
                src_ref=gath.at[me],
                dst_ref=gath.at[me],
                send_sem=all_send,
                recv_sem=all_recv,
                device_id=(n // n_col, n % n_col),
                device_id_type=MESH,
            ).start()

        return carry

    lax.fori_loop(0, total, send_top, 0)

    window[...] = jnp.zeros_like(window)
    placed[...] = jnp.zeros_like(placed)
    even, odd = boxes_of(4, 0)
    for b in range(16):
        window[(b // 4 + 1) * 6 + b % 4 + 1] = (odd if b % 2 else even)[b // 2]
    even, odd = boxes_of(4, 1)
    back[:, 0] = even
    back[:, 1] = odd
    load_near.wait()

    def adjoint_row(r, carry):
        for c in range(4):
            y = back[r * 2 + c // 2, c % 2].astype(BF16)
            parts = []
            for k in range(2):
                a = nn(y, near[0, r * 4 + c, k])
                b = nn(y, near[1, r * 4 + c, k])
                parts.append(a - swap(b))
            for o in range(9):
                place = (r + o // 3) * 6 + c + o % 3
                term = placed[place]
                for k in range(2):
                    term += jnp.where(codes[r, c, k] == o, 1.0, 0.0) * parts[k]
                placed[place] = term
        return carry

    lax.fori_loop(0, 4, adjoint_row, 0)

    def span(step):
        return {-1: [0], 0: [1, 2, 3, 4], 1: [5]}[step]

    def ring_copy(d):
        dr, dc = d // 3 - 1, d % 3 - 1
        size = 4 if dr == 0 or dc == 0 else 1
        return pltpu.make_async_remote_copy(
            src_ref=ring_out.at[d, pl.ds(0, size)],
            dst_ref=ring_in.at[8 - d, pl.ds(0, size)],
            send_sem=ring_send.at[d],
            recv_sem=ring_recv.at[8 - d],
            device_id=(row + dr, col + dc),
            device_id_type=MESH,
        )

    directions = [d for d in range(9) if d != 4]
    for d in directions:

        @pl.when(exists(d))
        def _(d=d):
            at = 0
            for r in span(d // 3 - 1):
                for c in span(d % 3 - 1):
                    ring_out[d, at] = placed[r * 6 + c]
                    at += 1
            ring_copy(d).start()

    def spread_table(jr, carry):
        for x in range(2):
            rows = leaf_tab[x, jr]
            for jc in range(15):
                tab[x, jr * 15 + jc] = jnp.broadcast_to(rows[jc : jc + 1], (8, 128))
        return carry

    lax.fori_loop(0, 15, spread_table, 0)
    for x in range(2):
        for jr in range(6, 9):
            for jc in range(6, 9):
                tab[x, jr * 15 + jc] = jnp.zeros((8, 128), F32)
    leaf[...] = jnp.zeros_like(leaf)

    def translate(br, bc):
        for s in range(2):

            def source_row(rr, acc, s=s):
                acc = list(acc)
                plain = [patt[s, 0, rr * 2 + cc // 2, cc % 2] for cc in range(4)]
                turned = [patt[s, 1, rr * 2 + cc // 2, cc % 2] for cc in range(4)]
                for r in range(4):
                    for dc in range(-3, 4):
                        at = (br * 4 + rr + 3 - r) * 15 + bc * 4 + dc + 3
                        if s == 1:
                            at = 224 - at
                        t_re = tab[0, at]
                        t_im = tab[1, at]
                        for c in range(4):
                            cc = c + dc
                            if 0 <= cc < 4:
                                acc[r * 4 + c] += t_re * plain[cc] + t_im * turned[cc]
                return tuple(acc)

            acc = lax.fori_loop(0, 4, source_row, tuple(leaf[s, b] for b in range(16)))
            for b in range(16):
                leaf[s, b] = acc[b]

    translate(1, 1)

    def side_block(d, carry):
        @pl.when(exists(d))
        def _():
            halo_copy(8 - d).wait_recv()
            patterns(d)
            translate(d // 3, d % 3)

        return carry

    lax.fori_loop(0, 9, side_block, 0)

    inner = {-1: [3], 0: [0, 1, 2, 3], 1: [0]}
    for d in directions:

        @pl.when(exists(d))
        def _(d=d):
            even, odd = boxes_of(d, 0)
            for i, r in enumerate(inner[d // 3 - 1]):
                for j, c in enumerate(inner[d % 3 - 1]):
                    place = span(d // 3 - 1)[i] * 6 + span(d % 3 - 1)[j]
                    window[place] = (odd if c % 2 else even)[r * 2 + c // 2]

    def forward_row(r, carry):
        for c in range(4):
            a = jnp.zeros((8, 128), F32)
            b = jnp.zeros((8, 128), F32)
            for k in range(2):
                code = codes[r, c, k]
                place = jnp.where(code == 9, 36, (r + code // 3) * 6 + c + code % 3)
                v = window[place].astype(BF16)
                a += nt(v, near[0, r * 4 + c, k])
                b += nt(v, near[1, r * 4 + c, k])
            near_fwd[r * 4 + c] = a + swap(b)
        return carry

    lax.fori_loop(0, 4, forward_row, 0)

    for d in directions:

        @pl.when(exists(d))
        def _(d=d):
            ring_copy(8 - d).wait_recv()
            at = 0
            rows = {-1: [1], 0: [1, 2, 3, 4], 1: [4]}
            for r in rows[d // 3 - 1]:
                for c in rows[d % 3 - 1]:
                    placed[r * 6 + c] += ring_in[d, at]
                    at += 1

    others = gath.at[pl.ds(0, total - 1)]
    pltpu.make_async_copy(others, others, all_recv).wait()

    def coarse_row(rp, carry):
        acc = list(carry)
        ri = row - rp + n_row - 1
        for ci in range(2 * n_col - 1):
            cp = col + n_col - 1 - ci
            there = (cp >= 0) & (cp < n_col)
            apart = (jnp.abs(row - rp) > 1) | (abs(ci - n_col + 1) > 1)
            weight = jnp.where(there & apart, 1.0, 0.0)
            values = gath[rp * n_col + jnp.clip(cp, 0, n_col - 1)].astype(F32)
            for s in range(2):
                rs = ri if s == 0 else 2 * (n_row - 1) - ri
                cs = ci if s == 0 else 2 * (n_col - 1) - ci
                t_re = coarse_tab[0, rs].astype(F32)[cs : cs + 1] * weight
                t_im = coarse_tab[1, rs].astype(F32)[cs : cs + 1] * (weight if s == 0 else -weight)
                v = values[8 * s : 8 * s + 8]
                acc[2 * s] += t_re * v
                acc[2 * s + 1] += t_im * v
        return tuple(acc)

    sums = lax.fori_loop(0, n_row, coarse_row, (jnp.zeros((8, 256), F32),) * 4)

    for s in range(2):
        arrived = sums[2 * s] + swap(sums[2 * s + 1])
        turned = swap(arrived)
        down = [trig[0, j : j + 1] * arrived - trig[1, j : j + 1] * turned for j in range(16)]
        spread = nn(jnp.concatenate(down, 0), interp[...], HIGH)
        incoming = (leaf[s].reshape(128, 128) + spread).astype(BF16)
        both = nn(incoming, w_rcv[s])
        far = both[:, :128].reshape(16, 8, 128) + swap(both[:, 128:].reshape(16, 8, 128))
        out = out_fwd if s == 0 else out_adj
        for j in range(8):
            pair = []
            for b in (2 * j, 2 * j + 1):
                close = near_fwd[b] if s == 0 else placed[(b // 4 + 1) * 6 + b % 4 + 1]
                pair.append(far[b] + close)
            low = upper((8, 128))
            out[0, j] = jnp.where(low, pair[0], pltpu.roll(pair[1], 4, 0))
            out[1, j] = jnp.where(low, pltpu.roll(pair[0], 4, 0), pair[1])

    for d in directions:

        @pl.when(exists(d))
        def _(d=d):
            halo_copy(d).wait_send()
            ring_copy(d).wait_send()

    pltpu.make_async_copy(others, others, all_send).wait()


def per_device(
    n_row,
    n_col,
    current,
    probe,
    near_list,
    near_blocks,
    radiation,
    reception,
    interp,
    phase,
    leaf_table,
    coarse_table,
):
    total = n_row * n_col
    vmem = pl.BlockSpec(memory_space=pltpu.VMEM)
    half = jax.ShapeDtypeStruct((2, 8, 8, 128), F32)
    dma = pltpu.SemaphoreType.DMA
    fwd, adj = pl.pallas_call(
        functools.partial(kernel, n_row, n_col),
        out_shape=(half, half),
        in_specs=[
            vmem,
            vmem,
            pl.BlockSpec(memory_space=pltpu.SMEM),
            pl.BlockSpec(memory_space=pl.ANY),
        ]
        + [vmem] * 6,
        out_specs=(vmem, vmem),
        scratch_shapes=[
            pltpu.VMEM((9, 256, 128), BF16),
            pltpu.VMEM((total, 16, 256), BF16),
            pltpu.VMEM((2, 16, 2, 128, 128), BF16),
            pltpu.VMEM((2, 128, 256), BF16),
            pltpu.VMEM((2, 128, 256), BF16),
            pltpu.VMEM((2, 225, 8, 128), F32),
            pltpu.VMEM((2, 2, 8, 2, 8, 128), F32),
            pltpu.VMEM((2, 16, 8, 128), F32),
            pltpu.VMEM((1, 2, 8, 256), F32),
            pltpu.VMEM((37, 8, 128), F32),
            pltpu.VMEM((36, 8, 128), F32),
            pltpu.VMEM((9, 4, 8, 128), F32),
            pltpu.VMEM((9, 4, 8, 128), F32),
            pltpu.VMEM((16, 8, 128), F32),
            pltpu.VMEM((8, 2, 8, 128), F32),
            pltpu.VMEM((2, 16, 256), F32),
            dma,
            dma((9,)),
            dma((9,)),
            dma((9,)),
            dma((9,)),
            dma,
            dma,
        ],
        compiler_params=pltpu.CompilerParams(
            collective_id=0, has_side_effects=True, vmem_limit_bytes=40 * 1024 * 1024
        ),
        name="operator",
    )(
        current.reshape(128, 128),
        probe.reshape(128, 128),
        near_list,
        near_blocks.reshape(2, 16, 2, 128, 128),
        radiation,
        reception,
        interp,
        phase,
        leaf_table,
        coarse_table,
    )
    return fwd.reshape(current.shape), adj.reshape(current.shape)


def solution(mesh):
    placed = (
        P(None, "row", "col", None, None),
        P(None, "row", "col", None, None),
        P("row", "col", None),
        P(None, "row", "col", None, None, None),
        P(),
        P(),
        P(),
        P(),
        P(),
        P(),
    )
    return jax.shard_map(
        functools.partial(per_device, mesh.shape["row"], mesh.shape["col"]),
        mesh=mesh,
        in_specs=placed,
        out_specs=(P(None, "row", "col", None, None), P(None, "row", "col", None, None)),
        check_vma=False,
    )
```

time: 243 us -> 33.8 us (0.14)
  the two profiles are of different devices: /device:TPU:0 before, /device:TPU:3 now
where the time goes in v1:
time: 33.8 us; the launch traced here: 33.3 us
  Pallas kernels  22.3 us (66%)
  local copies, waits for them, and re-layouts  10.4 us (31%)
  between operations  0.66 us (2%)
    pallas_call x1, Pallas kernels, per_device(): pl.pallas_call(functools.partial(kernel, n_row, n_col), out_shape=(half,...  22.3 us
    unnamed x19, local copies, waits for them, and re-layouts  10.4 us

profile of v1, /device:TPU:3, one launch (start us, length us, event | category | flops | bytes accessed | tf_op | source)
XLA Modules:
  0.0 33.3 jit_solution(15739631578092845506)
XLA Ops:
  0.6 0.8 %copy.12.codes = s32[4,4,2]{2,1,0:T(4,128)S(1)} copy(s32[4,4,2]{1,2,0:T(2,128)} %param.12) | data formatting | bytes 256 | tf_op args[2]
  1.4 0.9 %copy.14.coarse_tab = bf16[2,31,3,256]{3,2,1,0:T(4,128)(2,1)S(1)} copy(bf16[2,31,3,256]{3,0,2,1:T(2,128)(2,1)} %param.19) | data formatting | bytes 190464 | tf_op args[9]
  2.4 1.0 %copy.13.leaf_tab = f32[2,15,15,128]{3,2,1,0:T(8,128)S(1)} copy(f32[2,15,15,128]{3,0,2,1:T(2,128)} %param.18) | data formatting | bytes 460800 | tf_op args[8]
  3.3 0.0 copy-start
  3.3 1.6 %copy-done = bf16[2,4,4,2,128,128]{5,4,3,2,1,0:T(8,128)(2,1)S(1)} copy-done((bf16[2,4,4,2,128,128]{5,4,3,2,1,0:T(8,128)(2,1)S(1)}, bf16[2,4,4,2,128,128]{5,4,3,2,1,0:T(8,128)(2,1)}, u32[]{:S(2)}) %copy-start) | copy-done | bytes 2097176
  4.9 0.0 copy-start.1
  4.9 0.9 %copy-done.1 = f32[256,128]{1,0:T(8,128)S(1)} copy-done((f32[256,128]{1,0:T(8,128)S(1)}, f32[256,128]{1,0:T(8,128)}, u32[]{:S(2)}) %copy-start.1) | copy-done | bytes 131096
  5.8 0.0 copy-start.2
  5.8 0.8 %copy-done.2 = bf16[2,128,128]{2,1,0:T(8,128)(2,1)S(1)} copy-done((bf16[2,128,128]{2,1,0:T(8,128)(2,1)S(1)}, bf16[2,128,128]{2,1,0:T(8,128)(2,1)}, u32[]{:S(2)}) %copy-start.2) | copy-done | bytes 65560
  6.7 0.0 copy-start.3
  6.7 0.8 %copy-done.3 = bf16[2,128,128]{2,1,0:T(8,128)(2,1)S(1)} copy-done((bf16[2,128,128]{2,1,0:T(8,128)(2,1)S(1)}, bf16[2,128,128]{2,1,0:T(8,128)(2,1)}, u32[]{:S(2)}) %copy-start.3) | copy-done | bytes 65560
  7.5 0.0 copy-start.4
  7.5 0.8 %copy-done.4 = bf16[2,4,4,4,128]{4,3,2,1,0:T(4,128)(2,1)S(1)} copy-done((bf16[2,4,4,4,128]{4,3,2,1,0:T(4,128)(2,1)S(1)}, bf16[2,4,4,4,128]{4,3,2,1,0:T(4,128)(2,1)}, u32[]{:S(2)}) %copy-start.4) | copy-done | bytes 32792
  8.3 0.0 copy-start.5
  8.3 0.8 %copy-done.5 = bf16[2,4,4,4,128]{4,3,2,1,0:T(4,128)(2,1)S(1)} copy-done((bf16[2,4,4,4,128]{4,3,2,1,0:T(4,128)(2,1)S(1)}, bf16[2,4,4,4,128]{4,3,2,1,0:T(4,128)(2,1)}, u32[]{:S(2)}) %copy-start.5) | copy-done | bytes 32792
  9.0 0.0 copy-start.6
  9.0 0.7 %copy-done.6 = f32[16,256]{1,0:T(8,128)S(1)} copy-done((f32[16,256]{1,0:T(8,128)S(1)}, f32[16,256]{1,0:T(8,128)}, u32[]{:S(2)}) %copy-start.6) | copy-done | bytes 16408
  9.8 22.3 %operator.1 = (f32[2,8,8,128]{3,2,1,0:T(8,128)S(1)}, f32[2,8,8,128]{3,2,1,0:T(8,128)S(1)}) custom-call(bf16[128,128]{1,0:T(8,128)(2,1)S(1)} %bitcast.8, bf16[128,128]{1,0:T(8,128)(2,1)S(1)} %bitcast.9, s32[4,4,2]{2,1,0:T(4,128)S(1)} %copy.12.codes, bf16[2,16,2,128,128]{4,3,2,1,0:T(8,128)(2,1)S(1)} %bitcast.5, bf16[2,128,128]{2,1,0:T(8,128)(2,1)S(1)} %copy-done.2, ...), custom_call_target="tpu_custom_call" | custom-call | tf_op jit(solution)/shard_map/operator/pallas_call | solution.py:398
  32.0 0.6 %copy.17 = f32[2,4,4,4,128]{4,3,2,1,0:T(4,128)} copy(f32[2,4,4,4,128]{4,3,2,1,0:T(4,128)S(1)} %bitcast.7) | data formatting | bytes 131072
  32.7 0.6 %copy.18 = f32[2,4,4,4,128]{4,3,2,1,0:T(4,128)} copy(f32[2,4,4,4,128]{4,3,2,1,0:T(4,128)S(1)} %bitcast.6) | data formatting | bytes 131072
Async XLA Ops:
  3.3 1.6 %copy-start = (bf16[2,4,4,2,128,128]{5,4,3,2,1,0:T(8,128)(2,1)S(1)}, bf16[2,4,4,2,128,128]{5,4,3,2,1,0:T(8,128)(2,1)}, u32[]{:S(2)}) copy-start(bf16[2,4,4,2,128,128]{5,4,3,2,1,0:T(8,128)(2,1)} %param.13) | copy-start | bytes 6291460
  4.9 0.9 %copy-start.1 = (f32[256,128]{1,0:T(8,128)S(1)}, f32[256,128]{1,0:T(8,128)}, u32[]{:S(2)}) copy-start(f32[256,128]{1,0:T(8,128)} %interp.1) | copy-start | bytes 393220
  5.8 0.8 %copy-start.2 = (bf16[2,128,128]{2,1,0:T(8,128)(2,1)S(1)}, bf16[2,128,128]{2,1,0:T(8,128)(2,1)}, u32[]{:S(2)}) copy-start(bf16[2,128,128]{2,1,0:T(8,128)(2,1)} %rad.1) | copy-start | bytes 196612
  6.7 0.8 %copy-start.3 = (bf16[2,128,128]{2,1,0:T(8,128)(2,1)S(1)}, bf16[2,128,128]{2,1,0:T(8,128)(2,1)}, u32[]{:S(2)}) copy-start(bf16[2,128,128]{2,1,0:T(8,128)(2,1)} %rec.1) | copy-start | bytes 196612
  7.5 0.8 %copy-start.4 = (bf16[2,4,4,4,128]{4,3,2,1,0:T(4,128)(2,1)S(1)}, bf16[2,4,4,4,128]{4,3,2,1,0:T(4,128)(2,1)}, u32[]{:S(2)}) copy-start(bf16[2,4,4,4,128]{4,3,2,1,0:T(4,128)(2,1)} %param.10) | copy-start | bytes 98308
  8.3 0.8 %copy-start.5 = (bf16[2,4,4,4,128]{4,3,2,1,0:T(4,128)(2,1)S(1)}, bf16[2,4,4,4,128]{4,3,2,1,0:T(4,128)(2,1)}, u32[]{:S(2)}) copy-start(bf16[2,4,4,4,128]{4,3,2,1,0:T(4,128)(2,1)} %param.11) | copy-start | bytes 98308
  9.0 0.7 %copy-start.6 = (f32[16,256]{1,0:T(8,128)S(1)}, f32[16,256]{1,0:T(8,128)}, u32[]{:S(2)}) copy-start(f32[16,256]{1,0:T(8,128)} %phase.1) | copy-start | bytes 49156

commit v2 on v1

--- a/solution.py
+++ b/solution.py
@@ -38,18 +38,24 @@
 def kernel(
     n_row,
     n_col,
-    cur,
-    prb,
+    cur_hbm,
+    prb_hbm,
     codes,
     near_hbm,
+    rad_hbm,
+    rec_hbm,
+    interp_hbm,
+    phase_hbm,
+    leaf_hbm,
+    coarse_hbm,
+    out_fwd,
+    out_adj,
     rad,
     rec,
     interp,
     phase,
     leaf_tab,
     coarse_tab,
-    out_fwd,
-    out_adj,
     halo,
     gath,
     near,
@@ -66,7 +72,7 @@
     near_fwd,
     back,
     trig,
-    near_sem,
+    load_sem,
     halo_send,
     halo_recv,
     ring_send,
@@ -79,6 +85,20 @@
     total = n_row * n_col
     me = row * n_col + col
 
+    moves = (
+        (cur_hbm, halo.at[4, pl.ds(0, 128)]),
+        (prb_hbm, halo.at[4, pl.ds(128, 128)]),
+        (rad_hbm, rad),
+        (rec_hbm, rec),
+        (interp_hbm, interp),
+        (phase_hbm, phase),
+        (near_hbm, near),
+        (leaf_hbm, leaf_tab),
+        (coarse_hbm, coarse_tab),
+    )
+    loads = [pltpu.make_async_copy(src, dst, load_sem.at[i]) for i, (src, dst) in enumerate(moves)]
+    for load in loads:
+        load.start()
     barrier = pltpu.get_barrier_semaphore()
 
     def greet(n, carry):
@@ -89,11 +109,9 @@
         return carry
 
     lax.fori_loop(0, total, greet, 0)
-    load_near = pltpu.make_async_copy(near_hbm, near, near_sem)
-    load_near.start()
-
-    halo[4, 0:128] = cur[...]
-    halo[4, 128:256] = prb[...]
+
+    for load in loads[:6]:
+        load.wait()
     for x in range(2):
         sign = 1.0 if x == 0 else -1.0
         cols = slice(128 * x, 128 * x + 128)
@@ -189,7 +207,7 @@
     even, odd = boxes_of(4, 1)
     back[:, 0] = even
     back[:, 1] = odd
-    load_near.wait()
+    loads[6].wait()
 
     def adjoint_row(r, carry):
         for c in range(4):
@@ -203,7 +221,7 @@
                 place = (r + o // 3) * 6 + c + o % 3
                 term = placed[place]
                 for k in range(2):
-                    term += jnp.where(codes[r, c, k] == o, 1.0, 0.0) * parts[k]
+                    term += jnp.where(codes[r, k, c] == o, 1.0, 0.0) * parts[k]
                 placed[place] = term
         return carry
 
@@ -236,11 +254,13 @@
                     at += 1
             ring_copy(d).start()
 
+    loads[7].wait()
+
     def spread_table(jr, carry):
-        for x in range(2):
-            rows = leaf_tab[x, jr]
-            for jc in range(15):
-                tab[x, jr * 15 + jc] = jnp.broadcast_to(rows[jc : jc + 1], (8, 128))
+        for jc in range(15):
+            rows = leaf_tab[jr, jc]
+            for x in range(2):
+                tab[x, jr * 15 + jc] = jnp.broadcast_to(rows[x : x + 1], (8, 128))
         return carry
 
     lax.fori_loop(0, 15, spread_table, 0)
@@ -303,7 +323,7 @@
             a = jnp.zeros((8, 128), F32)
             b = jnp.zeros((8, 128), F32)
             for k in range(2):
-                code = codes[r, c, k]
+                code = codes[r, k, c]
                 place = jnp.where(code == 9, 36, (r + code // 3) * 6 + c + code % 3)
                 v = window[place].astype(BF16)
                 a += nt(v, near[0, r * 4 + c, k])
@@ -328,20 +348,22 @@
     others = gath.at[pl.ds(0, total - 1)]
     pltpu.make_async_copy(others, others, all_recv).wait()
 
+    loads[8].wait()
+
     def coarse_row(rp, carry):
         acc = list(carry)
         ri = row - rp + n_row - 1
-        for ci in range(2 * n_col - 1):
-            cp = col + n_col - 1 - ci
-            there = (cp >= 0) & (cp < n_col)
-            apart = (jnp.abs(row - rp) > 1) | (abs(ci - n_col + 1) > 1)
-            weight = jnp.where(there & apart, 1.0, 0.0)
-            values = gath[rp * n_col + jnp.clip(cp, 0, n_col - 1)].astype(F32)
+        for cp in range(n_col):
+            ci = col - cp + n_col - 1
+            apart = (jnp.abs(row - rp) > 1) | (jnp.abs(col - cp) > 1)
+            weight = jnp.where(apart, 1.0, 0.0)
+            values = gath[rp * n_col + cp].astype(F32)
             for s in range(2):
                 rs = ri if s == 0 else 2 * (n_row - 1) - ri
                 cs = ci if s == 0 else 2 * (n_col - 1) - ci
-                t_re = coarse_tab[0, rs].astype(F32)[cs : cs + 1] * weight
-                t_im = coarse_tab[1, rs].astype(F32)[cs : cs + 1] * (weight if s == 0 else -weight)
+                coeff = coarse_tab[rs, cs].astype(F32)
+                t_re = coeff[0:1] * weight
+                t_im = coeff[1:2] * (weight if s == 0 else -weight)
                 v = values[8 * s : 8 * s + 8]
                 acc[2 * s] += t_re * v
                 acc[2 * s + 1] += t_im * v
@@ -393,20 +415,23 @@
 ):
     total = n_row * n_col
     vmem = pl.BlockSpec(memory_space=pltpu.VMEM)
+    hbm = pl.BlockSpec(memory_space=pltpu.HBM)
+    leaf_rows = jnp.transpose(leaf_table, (1, 2, 0, 3))
+    coarse_rows = jnp.transpose(coarse_table, (1, 2, 0, 3))
     half = jax.ShapeDtypeStruct((2, 8, 8, 128), F32)
     dma = pltpu.SemaphoreType.DMA
     fwd, adj = pl.pallas_call(
         functools.partial(kernel, n_row, n_col),
         out_shape=(half, half),
-        in_specs=[
-            vmem,
-            vmem,
-            pl.BlockSpec(memory_space=pltpu.SMEM),
-            pl.BlockSpec(memory_space=pl.ANY),
-        ]
-        + [vmem] * 6,
+        in_specs=[hbm, hbm, pl.BlockSpec(memory_space=pltpu.SMEM)] + [hbm] * 7,
         out_specs=(vmem, vmem),
         scratch_shapes=[
+            pltpu.VMEM(radiation.shape, BF16),
+            pltpu.VMEM(reception.shape, BF16),
+            pltpu.VMEM(interp.shape, F32),
+            pltpu.VMEM(phase.shape, F32),
+            pltpu.VMEM(leaf_rows.shape, F32),
+            pltpu.VMEM(coarse_rows.shape, BF16),
             pltpu.VMEM((9, 256, 128), BF16),
             pltpu.VMEM((total, 16, 256), BF16),
             pltpu.VMEM((2, 16, 2, 128, 128), BF16),
@@ -423,7 +448,7 @@
             pltpu.VMEM((16, 8, 128), F32),
             pltpu.VMEM((8, 2, 8, 128), F32),
             pltpu.VMEM((2, 16, 256), F32),
-            dma,
+            dma((9,)),
             dma((9,)),
             dma((9,)),
             dma((9,)),
@@ -432,20 +457,20 @@
             dma,
         ],
         compiler_params=pltpu.CompilerParams(
-            collective_id=0, has_side_effects=True, vmem_limit_bytes=40 * 1024 * 1024
+            collective_id=0, has_side_effects=True, vmem_limit_bytes=63 * 1024 * 1024
         ),
         name="operator",
     )(
         current.reshape(128, 128),
         probe.reshape(128, 128),
-        near_list,
+        jnp.transpose(near_list, (0, 2, 1)),
         near_blocks.reshape(2, 16, 2, 128, 128),
         radiation,
         reception,
         interp,
         phase,
-        leaf_table,
-        coarse_table,
+        leaf_rows,
+        coarse_rows,
     )
     return fwd.reshape(current.shape), adj.reshape(current.shape)
 

time: 33.8 us -> 26.8 us (0.79)
  local copies, waits for them, and re-layouts: 10.4 us -> 2.95 us
  Pallas kernels: 22.3 us -> 23 us
    unnamed x19 -> x2, local copies, waits for them, and re-layouts: 10.4 us -> 2.95 us
    pallas_call x1, Pallas kernels: 22.3 us -> 23 us  [per_device(): pl.pallas_call(functools.partial(kernel, n_row, n_col), out_shape=(half,...]
where the time goes in v2:
time: 26.8 us; the launch traced here: 26.6 us
  Pallas kernels  23 us (86%)
  local copies, waits for them, and re-layouts  2.95 us (11%)
  between operations  0.64 us (2%)
    pallas_call x1, Pallas kernels, per_device(): pl.pallas_call(functools.partial(kernel, n_row, n_col), out_shape=(half,...  23 us
    unnamed x2, local copies, waits for them, and re-layouts  2.95 us

profile of v2, /device:TPU:3, one launch (start us, length us, event | category | flops | bytes accessed | tf_op | source)
XLA Modules:
  0.0 26.6 jit_solution(11050488816123115289)
XLA Ops:
  0.6 23.0 %operator.1 = (f32[2,8,8,128]{3,2,1,0:T(8,128)}, f32[2,8,8,128]{3,2,1,0:T(8,128)}) custom-call(bf16[128,128]{1,0:T(8,128)(2,1)} %bitcast.13, bf16[128,128]{1,0:T(8,128)(2,1)} %bitcast.14, s32[4,2,4]{2,1,0:T(2,128)} %bitcast.15, bf16[2,16,2,128,128]{4,3,2,1,0:T(8,128)(2,1)} %bitcast.8, bf16[2,128,128]{2,1,0:T(8,128)(2,1)} %rad_hbm.1, ...), custom_call_target="tpu_custom_call" | custom-call | tf_op jit(solution)/shard_map/operator/pallas_call | solution.py:423
  23.6 1.5 %copy.14 = f32[2,4,4,4,128]{4,3,2,1,0:T(4,128)} copy(f32[2,4,4,4,128]{4,3,2,1,0:T(4,128)} %bitcast.12) | data formatting | bytes 131072
  25.1 1.5 %copy.15 = f32[2,4,4,4,128]{4,3,2,1,0:T(4,128)} copy(f32[2,4,4,4,128]{4,3,2,1,0:T(4,128)} %bitcast.11) | data formatting | bytes 131072

commit v3 on v2

--- a/solution.py
+++ b/solution.py
@@ -82,8 +82,6 @@
 ):
     row = lax.axis_index("row")
     col = lax.axis_index("col")
-    total = n_row * n_col
-    me = row * n_col + col
 
     moves = (
         (cur_hbm, halo.at[4, pl.ds(0, 128)]),
@@ -101,14 +99,60 @@
         load.start()
     barrier = pltpu.get_barrier_semaphore()
 
-    def greet(n, carry):
-        @pl.when(n != me)
+    def exists(d):
+        r = row + d // 3 - 1
+        c = col + d % 3 - 1
+        return (d != 4) & (r >= 0) & (r < n_row) & (c >= 0) & (c < n_col)
+
+    def greet(r, c):
+        pl.semaphore_signal(barrier, inc=1, device_id=(r, c), device_id_type=MESH)
+
+    def greet_rows(n, carry):
+        @pl.when(n != row)
         def _():
-            pl.semaphore_signal(barrier, inc=1, device_id=(n // n_col, n % n_col), device_id_type=MESH)
-
-        return carry
-
-    lax.fori_loop(0, total, greet, 0)
+            greet(n, col)
+
+        return carry
+
+    def greet_cols(n, carry):
+        @pl.when(n != col)
+        def _():
+            greet(row, n)
+
+        return carry
+
+    lax.fori_loop(0, n_row, greet_rows, 0)
+    lax.fori_loop(0, n_col, greet_cols, 0)
+    peers = n_row + n_col - 2
+    for d in (0, 2, 6, 8):
+        peers += jnp.where(exists(d), 1, 0)
+
+        @pl.when(exists(d))
+        def _(d=d):
+            greet(row + d // 3 - 1, col + d % 3 - 1)
+
+    pl.semaphore_wait(barrier, peers)
+
+    def halo_copies(d, to, slot, first):
+        sources = (cur_hbm, prb_hbm) if first else tuple(halo.at[d, pl.ds(128 * i, 128)] for i in range(2))
+        return [
+            pltpu.make_async_remote_copy(
+                src_ref=sources[i],
+                dst_ref=halo.at[slot, pl.ds(128 * i, 128)],
+                send_sem=halo_send.at[i, d + to - 4],
+                recv_sem=halo_recv.at[i, slot],
+                device_id=(row + to // 3 - 1, col + to % 3 - 1),
+                device_id_type=MESH,
+            )
+            for i in range(2)
+        ]
+
+    for d in (1, 7, 3, 5):
+
+        @pl.when(exists(d))
+        def _(d=d):
+            for copy in halo_copies(4, d, 8 - d, True):
+                copy.start()
 
     for load in loads[:6]:
         load.wait()
@@ -153,51 +197,26 @@
             sin_sum += trig[1, j : j + 1] * wide[j]
         top = cos_sum + swap(sin_sum)
         vec[0, s] = top
-    gath[me] = vec[0].reshape(16, 256).astype(BF16)
-
-    pl.semaphore_wait(barrier, total - 1)
-
-    def halo_copy(d):
-        dr = d // 3 - 1
-        dc = d % 3 - 1
+    gath[col, row] = vec[0].reshape(16, 256).astype(BF16)
+
+    def top_copy(r):
         return pltpu.make_async_remote_copy(
-            src_ref=halo.at[4],
-            dst_ref=halo.at[8 - d],
-            send_sem=halo_send.at[d],
-            recv_sem=halo_recv.at[8 - d],
-            device_id=(row + dr, col + dc),
+            src_ref=gath.at[col, row],
+            dst_ref=gath.at[col, row],
+            send_sem=all_send.at[0],
+            recv_sem=all_recv.at[0],
+            device_id=(r, col),
             device_id_type=MESH,
         )
 
-    def exists(d):
-        r = row + d // 3 - 1
-        c = col + d % 3 - 1
-        return (d != 4) & (r >= 0) & (r < n_row) & (c >= 0) & (c < n_col)
-
-    def send_halo(d, carry):
-        @pl.when(exists(d))
+    def send_top(n, carry):
+        @pl.when(n != row)
         def _():
-            halo_copy(d).start()
-
-        return carry
-
-    lax.fori_loop(0, 9, send_halo, 0)
-
-    def send_top(n, carry):
-        @pl.when(n != me)
-        def _():
-            pltpu.make_async_remote_copy(
-                src_ref=gath.at[me],
-                dst_ref=gath.at[me],
-                send_sem=all_send,
-                recv_sem=all_recv,
-                device_id=(n // n_col, n % n_col),
-                device_id_type=MESH,
-            ).start()
-
-        return carry
-
-    lax.fori_loop(0, total, send_top, 0)
+            top_copy(n).start()
+
+        return carry
+
+    lax.fori_loop(0, n_row, send_top, 0)
 
     window[...] = jnp.zeros_like(window)
     placed[...] = jnp.zeros_like(placed)
@@ -253,6 +272,19 @@
                     ring_out[d, at] = placed[r * 6 + c]
                     at += 1
             ring_copy(d).start()
+
+    for d in (1, 7):
+
+        @pl.when(exists(d))
+        def _(d=d):
+            for copy in halo_copies(4, d, d, False):
+                copy.wait_recv()
+            for to in (3, 5):
+
+                @pl.when(exists(to))
+                def _(to=to):
+                    for copy in halo_copies(d, to, d + 4 - to, False):
+                        copy.start()
 
     loads[7].wait()
 
@@ -296,16 +328,52 @@
 
     translate(1, 1)
 
-    def side_block(d, carry):
-        @pl.when(exists(d))
+    column = gath.at[0, pl.ds(0, n_row - 1)]
+    pltpu.make_async_copy(column, column, all_recv.at[0]).wait()
+
+    def send_column(n, carry):
+        @pl.when(n != col)
         def _():
-            halo_copy(8 - d).wait_recv()
-            patterns(d)
-            translate(d // 3, d % 3)
-
-        return carry
-
-    lax.fori_loop(0, 9, side_block, 0)
+            pltpu.make_async_remote_copy(
+                src_ref=gath.at[col],
+                dst_ref=gath.at[col],
+                send_sem=all_send.at[1],
+                recv_sem=all_recv.at[1],
+                device_id=(row, n),
+                device_id_type=MESH,
+            ).start()
+
+        return carry
+
+    lax.fori_loop(0, n_col, send_column, 0)
+
+    def side_block(d):
+        patterns(d)
+        translate(d // 3, d % 3)
+
+    def direct_block(i, carry):
+        d = 1 + 6 * i
+
+        @pl.when(exists(d))
+        def _():
+            side_block(d)
+
+        return carry
+
+    lax.fori_loop(0, 2, direct_block, 0)
+
+    def across_block(i, carry):
+        d = (i // 2 + 1) % 3 * 3 + i % 2 * 2
+
+        @pl.when(exists(d))
+        def _():
+            for copy in halo_copies(4, d, d, False):
+                copy.wait_recv()
+            side_block(d)
+
+        return carry
+
+    lax.fori_loop(0, 6, across_block, 0)
 
     inner = {-1: [3], 0: [0, 1, 2, 3], 1: [0]}
     for d in directions:
@@ -345,9 +413,8 @@
                     placed[r * 6 + c] += ring_in[d, at]
                     at += 1
 
-    others = gath.at[pl.ds(0, total - 1)]
-    pltpu.make_async_copy(others, others, all_recv).wait()
-
+    others = gath.at[pl.ds(0, n_col - 1)]
+    pltpu.make_async_copy(others, others, all_recv.at[1]).wait()
     loads[8].wait()
 
     def coarse_row(rp, carry):
@@ -357,7 +424,7 @@
             ci = col - cp + n_col - 1
             apart = (jnp.abs(row - rp) > 1) | (jnp.abs(col - cp) > 1)
             weight = jnp.where(apart, 1.0, 0.0)
-            values = gath[rp * n_col + cp].astype(F32)
+            values = gath[cp, rp].astype(F32)
             for s in range(2):
                 rs = ri if s == 0 else 2 * (n_row - 1) - ri
                 cs = ci if s == 0 else 2 * (n_col - 1) - ci
@@ -393,10 +460,12 @@
 
         @pl.when(exists(d))
         def _(d=d):
-            halo_copy(d).wait_send()
+            for copy in halo_copies(4, d, 8 - d, d % 2 == 1):
+                copy.wait_send()
             ring_copy(d).wait_send()
 
-    pltpu.make_async_copy(others, others, all_send).wait()
+    pltpu.make_async_copy(column, column, all_send.at[0]).wait()
+    pltpu.make_async_copy(others, others, all_send.at[1]).wait()
 
 
 def per_device(
@@ -413,12 +482,11 @@
     leaf_table,
     coarse_table,
 ):
-    total = n_row * n_col
     vmem = pl.BlockSpec(memory_space=pltpu.VMEM)
     hbm = pl.BlockSpec(memory_space=pltpu.HBM)
     leaf_rows = jnp.transpose(leaf_table, (1, 2, 0, 3))
     coarse_rows = jnp.transpose(coarse_table, (1, 2, 0, 3))
-    half = jax.ShapeDtypeStruct((2, 8, 8, 128), F32)
+    half = pltpu.VMEM((2, 8, 8, 128), F32)
     dma = pltpu.SemaphoreType.DMA
     fwd, adj = pl.pallas_call(
         functools.partial(kernel, n_row, n_col),
@@ -433,7 +501,7 @@
             pltpu.VMEM(leaf_rows.shape, F32),
             pltpu.VMEM(coarse_rows.shape, BF16),
             pltpu.VMEM((9, 256, 128), BF16),
-            pltpu.VMEM((total, 16, 256), BF16),
+            pltpu.VMEM((n_col, n_row, 16, 256), BF16),
             pltpu.VMEM((2, 16, 2, 128, 128), BF16),
             pltpu.VMEM((2, 128, 256), BF16),
             pltpu.VMEM((2, 128, 256), BF16),
@@ -449,12 +517,12 @@
             pltpu.VMEM((8, 2, 8, 128), F32),
             pltpu.VMEM((2, 16, 256), F32),
             dma((9,)),
+            dma((2, 9)),
+            dma((2, 9)),
             dma((9,)),
             dma((9,)),
-            dma((9,)),
-            dma((9,)),
-            dma,
-            dma,
+            dma((2,)),
+            dma((2,)),
         ],
         compiler_params=pltpu.CompilerParams(
             collective_id=0, has_side_effects=True, vmem_limit_bytes=63 * 1024 * 1024

time: 26.8 us -> 20.8 us (0.78)
  the two profiles are of different devices: /device:TPU:3 before, /device:TPU:0 now
where the time goes in v3:
time: 20.8 us; the launch traced here: 20.4 us
  Pallas kernels  18.5 us (89%)
  local copies, waits for them, and re-layouts  1.26 us (6%)
  between operations  0.64 us (3%)
    pallas_call x1, Pallas kernels, per_device(): pl.pallas_call(functools.partial(kernel, n_row, n_col), out_shape=(half,...  18.5 us
    unnamed x2, local copies, waits for them, and re-layouts  1.26 us

profile of v3, /device:TPU:0, one launch (start us, length us, event | category | flops | bytes accessed | tf_op | source)
XLA Modules:
  0.0 20.4 jit_solution(2344800234659101910)
XLA Ops:
  0.6 18.5 %operator.1 = (f32[2,8,8,128]{3,2,1,0:T(8,128)S(1)}, f32[2,8,8,128]{3,2,1,0:T(8,128)S(1)}) custom-call(bf16[128,128]{1,0:T(8,128)(2,1)} %bitcast.13, bf16[128,128]{1,0:T(8,128)(2,1)} %bitcast.14, s32[4,2,4]{2,1,0:T(2,128)} %bitcast.15, bf16[2,16,2,128,128]{4,3,2,1,0:T(8,128)(2,1)} %bitcast.10, bf16[2,128,128]{2,1,0:T(8,128)(2,1)} %rad_hbm.1, ...), custom_call_target="tpu_custom_call" | custom-call | tf_op jit(solution)/shard_map/operator/pallas_call | solution.py:491
  19.2 0.6 %copy.14 = f32[2,4,4,4,128]{4,3,2,1,0:T(4,128)} copy(f32[2,4,4,4,128]{4,3,2,1,0:T(4,128)S(1)} %bitcast.9) | data formatting | bytes 131072
  19.8 0.6 %copy.15 = f32[2,4,4,4,128]{4,3,2,1,0:T(4,128)} copy(f32[2,4,4,4,128]{4,3,2,1,0:T(4,128)S(1)} %bitcast.8) | data formatting | bytes 131072

commit v4 on v3

--- a/solution.py
+++ b/solution.py
@@ -95,8 +95,6 @@
         (coarse_hbm, coarse_tab),
     )
     loads = [pltpu.make_async_copy(src, dst, load_sem.at[i]) for i, (src, dst) in enumerate(moves)]
-    for load in loads:
-        load.start()
     barrier = pltpu.get_barrier_semaphore()
 
     def exists(d):
@@ -131,6 +129,8 @@
         def _(d=d):
             greet(row + d // 3 - 1, col + d % 3 - 1)
 
+    for load in loads:
+        load.start()
     pl.semaphore_wait(barrier, peers)
 
     def halo_copies(d, to, slot, first):

time: 20.8 us -> 20.9 us (level)
  no operation moved by 1% of the time
where the time goes in v4:
time: 20.9 us; the launch traced here: 20.4 us
  Pallas kernels  18.5 us (89%)
  local copies, waits for them, and re-layouts  1.26 us (6%)
  between operations  0.64 us (3%)
    pallas_call x1, Pallas kernels, per_device(): pl.pallas_call(functools.partial(kernel, n_row, n_col), out_shape=(half,...  18.5 us
    unnamed x2, local copies, waits for them, and re-layouts  1.26 us

profile of v4, /device:TPU:0, one launch (start us, length us, event | category | flops | bytes accessed | tf_op | source)
XLA Modules:
  0.0 20.4 jit_solution(17331186972431550717)
XLA Ops:
  0.6 18.5 %operator.1 = (f32[2,8,8,128]{3,2,1,0:T(8,128)S(1)}, f32[2,8,8,128]{3,2,1,0:T(8,128)S(1)}) custom-call(bf16[128,128]{1,0:T(8,128)(2,1)} %bitcast.13, bf16[128,128]{1,0:T(8,128)(2,1)} %bitcast.14, s32[4,2,4]{2,1,0:T(2,128)} %bitcast.15, bf16[2,16,2,128,128]{4,3,2,1,0:T(8,128)(2,1)} %bitcast.10, bf16[2,128,128]{2,1,0:T(8,128)(2,1)} %rad_hbm.1, ...), custom_call_target="tpu_custom_call" | custom-call | tf_op jit(solution)/shard_map/operator/pallas_call | solution.py:491
  19.2 0.6 %copy.14 = f32[2,4,4,4,128]{4,3,2,1,0:T(4,128)} copy(f32[2,4,4,4,128]{4,3,2,1,0:T(4,128)S(1)} %bitcast.9) | data formatting | bytes 131072
  19.8 0.6 %copy.15 = f32[2,4,4,4,128]{4,3,2,1,0:T(4,128)} copy(f32[2,4,4,4,128]{4,3,2,1,0:T(4,128)S(1)} %bitcast.8) | data formatting | bytes 131072
